TPU v7x, 32 devices: a whole 2x2x4 slice. The times are simulated.
32 devices in a mesh: grp: 2 (over x), shot: 8 (over z, y), depth: 2 (over core).
Axes of the slice: x: 2, y: 2, z: 4, core: 2. Of those that a mesh axis runs over, the one named last changes fastest.
Arguments:
- wave_prev: float32 [16, 32, 128, 128], P(('grp', 'shot'), 'depth'), parts along dimension 0, may hold values from -6 to 6
- wave_now: float32 [16, 32, 128, 128], P(('grp', 'shot'), 'depth'), parts along dimension 0, may hold values from -6 to 6
- adjoint: float32 [16, 4, 32, 128, 128], P(('grp', 'shot'), None, 'depth'), parts along dimension 0, may hold values from -6 to 6
- coarse_velocity: float32 [32, 4096], P(('grp', 'depth'), 'shot'), parts along dimension 0, may hold values from 1.5 to 4.5
- filters: float32 [16, 27], replicated, may hold values from -1.25 to 1.25
- wavelet: float32 [16, 4], P(('grp', 'shot')), parts along dimension 0, may hold values from -30 to 30
- source_cell: int32 [16], P(('grp', 'shot')), parts along dimension 0, may hold values from 0 to 524287
- receiver_cells: int32 [16, 128], P(('grp', 'shot')), parts along dimension 0, may hold values from 0 to 524287
Outputs:
- gradient: float32 [32, 4096], P(('grp', 'depth'), 'shot'), parts along dimension 0
- wave_prev_out: float32 [16, 32, 128, 128], P(('grp', 'shot'), 'depth'), parts along dimension 0
- wave_now_out: float32 [16, 32, 128, 128], P(('grp', 'shot'), 'depth'), parts along dimension 0
- traces: float32 [16, 4, 128], P(('grp', 'shot')), parts along dimension 0
There are 2 independent parts, one for each index of `grp`. A program takes and returns all parts, laid end to end along the dimension named above; an argument that names none is the same for every part. Nothing has to cross between parts.
All inputs are finite; a program needn't handle non-finite values.
Results may differ from a plain program's by a relative error of at most 0.0003.
Values sent between devices are 32-bit elements; how exact they have to be, the bound alone decides.
A program may use at most 192 MiB of HBM per device.

v0:
```python
import functools

import jax
import jax.numpy as jnp
from jax import lax
from jax.experimental import pallas as pl
from jax.experimental.pallas import tpu as pltpu
from jax.sharding import PartitionSpec as P

coeffs = (-205.0 / 72.0, 8.0 / 5.0, -1.0 / 5.0, 8.0 / 315.0, -1.0 / 560.0)
courant = 0.1
HALO = 4
f32, bf16, i32 = jnp.float32, jnp.bfloat16, jnp.int32
NT = (((1,), (1,)), ((), ()))
TN = (((0,), (0,)), ((), ()))


def iota(shape, dim):
    return lax.broadcasted_iota(i32, shape, dim)


def split(value, parts):
    out = []
    for _ in range(parts - 1):
        part = value.astype(bf16)
        value = value - part.astype(f32)
        out.append(part)
    return out + [value.astype(bf16)]


def mm(a, b):
    return jnp.dot(a, b, preferred_element_type=f32)


def kernel(
    shots, steps,
    prev_hbm, now_hbm, adj_hbm, cv, filt, wav, src, rec_s, rec_v,
    grad, pout, nout, traces,
    *scratch,
):
    fields = scratch[: steps + 2]
    adjs = scratch[steps + 2 : 2 * steps + 2]
    (
        speed, acc, bx, by, lat, vel, velf, wown, wother, zx, xm, fhi, flo, sb,
        tmp, terms, arrived, picked, tr_own, tr_other,
        in_sem, out_sem, h_send, h_recv, v_send, v_recv, r_send, r_recv, w_sem, t_sem,
    ) = scratch[2 * steps + 2 :]
    rows, wx, wy = adjs[0].shape
    zc_rows, ncol = cv.shape
    half_y = wy // 2
    tiles = ncol // wy
    pairs_x = shots * tiles
    chans = filt.shape[0]
    me_s, me_d = lax.axis_index("shot"), lax.axis_index("depth")
    other = {"depth": 1 - me_d}
    MESH = pl.DeviceIdType.MESH

    def peer(k):
        return lax.rem(me_s + k, shots)

    load_now = pltpu.make_async_copy(now_hbm.at[0], fields[1].at[pl.ds(HALO, rows)], in_sem.at[0])
    load_prev = pltpu.make_async_copy(prev_hbm.at[0], fields[0].at[pl.ds(HALO, rows)], in_sem.at[1])
    load_adj = [
        pltpu.make_async_copy(adj_hbm.at[0, t], adjs[t], in_sem.at[2 + t]) for t in range(steps)
    ]
    load_now.start()
    load_prev.start()
    for c in load_adj:
        c.start()

    barrier = pltpu.get_barrier_semaphore()
    for k in range(1, shots):
        pl.semaphore_signal(barrier, inc=1, device_id={"shot": peer(k)}, device_id_type=MESH)
    pl.semaphore_signal(barrier, inc=1, device_id=other, device_id_type=MESH)
    pl.semaphore_wait(barrier, shots)

    def vel_copy(k, slot, to):
        return pltpu.make_async_remote_copy(
            src_ref=cv, dst_ref=vel.at[slot], send_sem=v_send.at[k], recv_sem=v_recv.at[k],
            device_id={"shot": to}, device_id_type=MESH,
        )

    for k in range(1, shots):
        vel_copy(k, me_s, peer(k)).start()
    inner = jnp.where(me_d == 0, rows - HALO, 0)
    far = jnp.where(me_d == 0, 0, rows + HALO)
    first_halo = pltpu.make_async_remote_copy(
        src_ref=now_hbm.at[0, pl.ds(inner, HALO)], dst_ref=fields[1].at[pl.ds(far, HALO)],
        send_sem=h_send.at[0], recv_sem=h_recv.at[0], device_id=other, device_id_type=MESH,
    )
    first_halo.start()

    for t in range(steps):
        fields[t + 1][pl.ds(far, HALO)] = jnp.zeros((HALO, wx, wy), f32)
    gap_x = jnp.abs(iota((wx, wx), 0) - iota((wx, wx), 1))
    gap_y = jnp.abs(iota((wy, wy), 0) - iota((wy, wy), 1))

    def band(gap):
        value = jnp.where(gap == 0, 1.5 * coeffs[0], 0.0).astype(f32)
        for k in range(1, 5):
            value = jnp.where(gap == k, coeffs[k], value)
        return split(value, 2)

    high, low = band(gap_x)
    bx[...] = jnp.concatenate([high, high, low], axis=1)
    high, low = band(gap_y)
    by[...] = jnp.concatenate([high, high, low], axis=0)

    width = chans * half_y
    spread = (iota((chans, width), 1) // half_y == iota((chans, width), 0)).astype(f32)
    taps = lax.dot_general(
        filt[...], spread, TN, precision=lax.Precision.HIGHEST, preferred_element_type=f32
    )
    taps_hi = taps.astype(bf16).astype(f32)
    taps_lo = taps - taps_hi
    shift_y = iota((half_y, width), 0) - iota((half_y, width), 1) % half_y
    for ab in range(9):
        for weights, out in ((taps_hi, fhi), (taps_lo, flo)):
            value = jnp.zeros((half_y, width), f32)
            for e in (-1, 0, 1):
                value = jnp.where(shift_y == e, weights[3 * ab + e + 1 : 3 * ab + e + 2], value)
            value = value.astype(bf16)
            out[pl.ds(ab * wy, half_y), :] = value
            out[pl.ds(ab * wy + half_y, half_y), :] = value

    vel[pl.ds(me_s, 1)] = cv[...][None]
    for k in range(1, shots):
        from_s = lax.rem(me_s + shots - k, shots)
        vel_copy(k, from_s, peer(k)).wait_recv()
    stacked = jnp.concatenate(
        [vel[s, :, q * wy : (q + 1) * wy] for s in range(shots) for q in range(tiles)], axis=0
    )
    up_row, up_col = iota((wy, 2 * wy), 0), iota((wy, 2 * wy), 1)
    up = (up_row == up_col // wy * half_y + up_col % wy // 2).astype(f32).astype(bf16)
    fine = mm(
        jnp.concatenate(split(stacked, 3), axis=1), jnp.concatenate([up, up, up], axis=0)
    )
    velf[0] = fine[:, :wy]
    velf[1] = fine[:, wy:]
    for z in range(zc_rows):
        for i in range(2):
            plane = courant * velf[i, pl.ds(z, pairs_x, stride=zc_rows), :]
            plane = plane * plane
            for j in range(2):
                speed[z, pl.ds(2 * i + j, pairs_x, stride=4), :] = plane

    before = vel[jnp.maximum(me_s - 1, 0), :, ncol - wy :]
    after = vel[jnp.minimum(me_s + 1, shots - 1), :, :wy]
    wown[0] = jnp.where(me_s > 0, before, 0.0)
    for q in range(tiles):
        wown[q + 1] = cv[:, q * wy : (q + 1) * wy]
    wown[tiles + 1] = jnp.where(me_s < shots - 1, after, 0.0)
    w_copy = pltpu.make_async_remote_copy(
        src_ref=wown, dst_ref=wother, send_sem=w_sem.at[0], recv_sem=w_sem.at[1],
        device_id=other, device_id_type=MESH,
    )
    w_copy.start()

    hit = src[0]
    hit_z = hit // (wx * wy) - me_d * rows
    hit_x = hit // wy % wx
    hit_y = hit % wy
    spot = ((iota((wx, wy), 0) == hit_x) & (iota((wx, wy), 1) == hit_y)).astype(f32)
    tmp[...] = spot
    chunk = 32

    def pair(t, zc):
        current, earlier, following = fields[t + 1], fields[t], fields[t + 2]
        z0 = 2 * zc
        halves = [split(current[z0 + HALO + i], 2) for i in range(2)]
        wide = [jnp.concatenate([halves[0][h], halves[1][h]], axis=1) for h in range(2)]
        tall = [jnp.concatenate([halves[0][h], halves[1][h]], axis=0) for h in range(2)]
        along_x = mm(bx[...], jnp.concatenate([wide[0], wide[1], wide[0]], axis=0))
        along_y = mm(jnp.concatenate([tall[0], tall[1], tall[0]], axis=1), by[...])
        for i in range(2):
            lat[i] = along_x[:, i * wy : (i + 1) * wy] + along_y[i * wx : (i + 1) * wx]
        for r in range(0, wx, chunk):
            cut = pl.ds(r, chunk)
            speed_cut = speed[zc, cut, :]
            spot_cut = tmp[cut, :]
            image = None
            planes = [current[z0 + k, cut, :] for k in range(2 * HALO + 2)]
            for i in range(2):
                pulse = jnp.where(hit_z == z0 + i, wav[0, t], 0.0)
                lap = lat[i, cut, :] + spot_cut * pulse
                for k in range(1, 5):
                    lap = lap + coeffs[k] * (planes[i + HALO + k] + planes[i + HALO - k])
                following[z0 + i + HALO, cut, :] = (
                    2.0 * planes[i + HALO] - earlier[z0 + i + HALO, cut, :] + speed_cut * lap
                )
                term = adjs[t][z0 + i, cut, :] * lap
                image = term if image is None else image + term
            if t == 0:
                acc[zc, cut, :] = image
            else:
                acc[zc, cut, :] = acc[zc, cut, :] + image

    edge_pairs = HALO // 2
    inside_pairs = rows // 2 - edge_pairs
    inside_first = me_d * edge_pairs
    edge_first = jnp.where(me_d == 0, inside_pairs, 0)
    halo = first_halo
    sent = [first_halo]
    load_now.wait()
    load_prev.wait()
    stores = []
    for t in range(steps):
        load_adj[t].wait()

        @pl.loop(0, inside_pairs)
        def _(i):
            pair(t, inside_first + i)

        halo.wait_recv()

        @pl.loop(0, edge_pairs)
        def _(i):
            pair(t, edge_first + i)

        if t + 1 < steps:
            halo = pltpu.make_async_remote_copy(
                src_ref=fields[t + 2].at[pl.ds(inner + HALO, HALO)],
                dst_ref=fields[t + 2].at[pl.ds(far, HALO)],
                send_sem=h_send.at[t + 1], recv_sem=h_recv.at[t + 1],
                device_id=other, device_id_type=MESH,
            )
            halo.start()
            sent.append(halo)
        if t + 2 >= steps:
            out = pout if t + 2 == steps else nout
            store = pltpu.make_async_copy(
                fields[t + 2].at[pl.ds(HALO, rows)], out.at[0], out_sem.at[t + 2 - steps]
            )
            store.start()
            stores.append(store)

    fold_row, fold_col = iota((wy, wy), 0), iota((wy, wy), 1)
    fold = (fold_row // 2 == fold_col % half_y).astype(f32).astype(bf16)
    fold = jnp.concatenate([fold, fold], axis=0)
    left = iota((1, wy), 1) < half_y
    for z in range(zc_rows):
        tmp[...] = mm(jnp.concatenate(split(acc[z], 2), axis=1), fold)
        quarter = [tmp[pl.ds(j, pairs_x, stride=4), :] for j in range(4)]
        terms[pl.ds(z, pairs_x, stride=zc_rows), :] = jnp.where(
            left, quarter[0] + quarter[1], quarter[2] + quarter[3]
        )
    block = tiles * zc_rows

    def term_copy(k, slot, to):
        return pltpu.make_async_remote_copy(
            src_ref=terms.at[pl.ds(pl.multiple_of(to * block, 8), block)],
            dst_ref=arrived.at[slot], send_sem=r_send.at[k], recv_sem=r_recv.at[k],
            device_id={"shot": to}, device_id_type=MESH,
        )

    for k in range(1, shots):
        term_copy(k, me_s, peer(k)).start()

    plane_size = wx * wy
    top = rows * plane_size - 1

    @pl.loop(0, rec_s.shape[1])
    def _(r):
        cell = jnp.clip(rec_s[0, r] - me_d * rows * plane_size, 0, top)
        z, x = cell // plane_size, cell // wy % wx
        for t in range(steps):
            picked[t, pl.ds(r, 1), :] = fields[t + 2][z + HALO, pl.ds(x, 1), :]

    cells = rec_v[...] - me_d * rows * plane_size
    inside = (cells >= 0) & (cells <= top)
    count = rec_s.shape[1]
    lane_hit = (iota((wy, count), 0) == jnp.clip(cells, 0, top) % wy) & inside
    tr_own[...] = jnp.zeros_like(tr_own)
    for t in range(steps):
        flipped = jnp.where(lane_hit, picked[t].T, 0.0)
        tr_own[pl.ds(t, 1), :] = jnp.sum(flipped, axis=0, keepdims=True)
    t_copy = pltpu.make_async_remote_copy(
        src_ref=tr_own, dst_ref=tr_other, send_sem=t_sem.at[0], recv_sem=t_sem.at[1],
        device_id=other, device_id_type=MESH,
    )
    t_copy.start()

    w_copy.wait_recv()
    for g in range(tiles + 2):
        own, near = wown[g], wother[g]
        tall = jnp.concatenate(
            [jnp.where(me_d == 0, 0.0, near), own, jnp.where(me_d == 0, near, 0.0)], axis=0
        )
        turned = pltpu.roll(tall, half_y, axis=1)
        for i, both in enumerate((jnp.where(left, tall, turned), jnp.where(left, turned, tall))):
            part = both.astype(bf16).astype(f32)
            zx[2 * g + i] = jnp.where(left, part, both - part)
    out_x = 2 * tiles + 2
    deep = 2 * zc_rows

    @pl.loop(0, out_x)
    def _(j):
        for a in range(3):
            for b in range(3):
                ab = 3 * a + b
                xm[pl.ds(pl.multiple_of(j * deep, 16), deep), ab * wy : (ab + 1) * wy] = zx[
                    j + b, zc_rows - 2 + a : zc_rows - 2 + a + deep, :
                ].astype(bf16)

    scores = mm(xm[...], fhi[...]) + mm(xm[...], flo[...])
    line = iota((out_x * deep, 1), 0)
    line_x, line_z = line // deep, line % deep
    good = (
        ((line_z > 0) | (me_d > 0))
        & ((line_z <= zc_rows) | (me_d == 0))
        & ((line_x > 0) | (me_s > 0))
        & ((line_x < out_x - 1) | (me_s < shots - 1))
    )
    response = jnp.where(good, scores / (1.0 + scores * scores), 0.0)
    res_hi, res_lo = split(response, 2)

    def nt(a, b):
        return lax.dot_general(a, b, NT, preferred_element_type=f32)

    sb[...] = nt(res_hi, fhi[...]) + nt(res_lo, fhi[...]) + nt(res_hi, flo[...])

    for k in range(1, shots):
        from_s = lax.rem(me_s + shots - k, shots)
        term_copy(k, from_s, peer(k)).wait_recv()
    for q in range(tiles):
        sides = []
        for i in range(2):
            x = 2 * q + i
            value = None
            for a in (-1, 0, 1):
                for b in (-1, 0, 1):
                    ab = 3 * (a + 1) + b + 1
                    piece = sb[
                        pl.ds((x + 1 - b) * deep + 1 - a, zc_rows), ab * wy : (ab + 1) * wy
                    ]
                    value = piece if value is None else value + piece
            sides.append(value)
        total = terms[pl.ds(pl.multiple_of(me_s * block, 8) + q * zc_rows, zc_rows), :]
        for k in range(1, shots):
            total = total + arrived[
                lax.rem(me_s + shots - k, shots), q * zc_rows : (q + 1) * zc_rows, :
            ]
        cut = slice(q * wy, (q + 1) * wy)
        scale = -2.0 * courant * courant / cv[:, cut]
        grad[:, cut] = total * scale + jnp.where(left, sides[0], sides[1])
    t_copy.wait_recv()
    traces[0] = tr_own[:steps] + tr_other[:steps]

    for k in range(1, shots):
        vel_copy(k, me_s, peer(k)).wait_send()
        term_copy(k, me_s, peer(k)).wait_send()
    for c in sent:
        c.wait_send()
    w_copy.wait_send()
    t_copy.wait_send()
    for c in stores:
        c.wait()


def body(
    shots, wave_prev, wave_now, adjoint, coarse_velocity, filters, wavelet, source_cell,
    receiver_cells,
):
    _, steps, rows, wx, wy = adjoint.shape
    zc_rows, ncol = coarse_velocity.shape
    half_y = wy // 2
    tiles = ncol // wy
    pairs_x = shots * tiles
    chans = filters.shape[0]
    count = receiver_cells.shape[1]
    out_x, deep = 2 * tiles + 2, 2 * zc_rows
    vmem = pl.BlockSpec(memory_space=pltpu.VMEM)
    smem = pl.BlockSpec(memory_space=pltpu.SMEM)
    anyw = pl.BlockSpec(memory_space=pl.ANY)
    trace_rows = -(-steps // 8) * 8
    dma = pltpu.SemaphoreType.DMA
    field = pltpu.VMEM((rows + 2 * HALO, wx, wy), f32)
    scratch = (
        [field] * (steps + 2)
        + [pltpu.VMEM((rows, wx, wy), f32)] * steps
        + [
            pltpu.VMEM((zc_rows, wx, wy), f32),
            pltpu.VMEM((zc_rows, wx, wy), f32),
            pltpu.VMEM((wx, 3 * wx), bf16),
            pltpu.VMEM((3 * wy, wy), bf16),
            pltpu.VMEM((2, wx, wy), f32),
            pltpu.VMEM((shots, zc_rows, ncol), f32),
            pltpu.VMEM((2, pairs_x * zc_rows, wy), f32),
            pltpu.VMEM((tiles + 2, zc_rows, wy), f32),
            pltpu.VMEM((tiles + 2, zc_rows, wy), f32),
            pltpu.VMEM((2 * tiles + 4, 3 * zc_rows, wy), f32),
            pltpu.VMEM((out_x * deep, 9 * wy), bf16),
            pltpu.VMEM((9 * wy, chans * half_y), bf16),
            pltpu.VMEM((9 * wy, chans * half_y), bf16),
            pltpu.VMEM((out_x * deep, 9 * wy), f32),
            pltpu.VMEM((wx, wy), f32),
            pltpu.VMEM((pairs_x * zc_rows, wy), f32),
            pltpu.VMEM((shots, tiles * zc_rows, wy), f32),
            pltpu.VMEM((steps, count, wy), f32),
            pltpu.VMEM((trace_rows, count), f32),
            pltpu.VMEM((trace_rows, count), f32),
            dma((2 + steps,)),
            dma((2,)),
            dma((steps,)),
            dma((steps,)),
            dma((shots,)),
            dma((shots,)),
            dma((shots,)),
            dma((shots,)),
            dma((2,)),
            dma((2,)),
        ]
    )
    return pl.pallas_call(
        functools.partial(kernel, shots, steps),
        out_shape=(
            jax.ShapeDtypeStruct((zc_rows, ncol), f32),
            jax.ShapeDtypeStruct(wave_prev.shape, f32),
            jax.ShapeDtypeStruct(wave_now.shape, f32),
            jax.ShapeDtypeStruct((1, steps, count), f32),
        ),
        in_specs=[anyw, anyw, anyw, vmem, vmem, smem, smem, smem, vmem],
        out_specs=(vmem, anyw, anyw, vmem),
        scratch_shapes=scratch,
        compiler_params=pltpu.CompilerParams(
            collective_id=0, has_side_effects=True, vmem_limit_bytes=52 * 2**20
        ),
    )(
        wave_prev, wave_now, adjoint, coarse_velocity, filters, wavelet, source_cell,
        receiver_cells, receiver_cells,
    )


def solution(mesh):
    return jax.shard_map(
        functools.partial(body, mesh.shape["shot"]),
        mesh=mesh,
        in_specs=(
            P(("grp", "shot"), "depth", None, None),
            P(("grp", "shot"), "depth", None, None),
            P(("grp", "shot"), None, "depth", None, None),
            P(("grp", "depth"), "shot"),
            P(),
            P(("grp", "shot"), None),
            P(("grp", "shot")),
            P(("grp", "shot"), None),
        ),
        out_specs=(
            P(("grp", "depth"), "shot"),
            P(("grp", "shot"), "depth", None, None),
            P(("grp", "shot"), "depth", None, None),
            P(("grp", "shot"), None, None),
        ),
        check_vma=False,
    )
```

profile of v0, /device:TPU:0, one launch (start us, length us, event | category | flops | bytes accessed | tf_op | source)
XLA Modules:
  0.0 34.8 jit_solution(11583783541516999694)
XLA Ops:
  1.3 0.0 copy-start
  1.3 0.7 %copy-done = f32[8,512]{1,0:T(8,128)S(1)} copy-done((f32[8,512]{1,0:T(8,128)S(1)}, f32[8,512]{1,0:T(8,128)}, u32[]{:S(2)}) %copy-start) | copy-done | bytes 16408
  2.0 0.0 copy-start.1
  2.0 0.7 %copy-done.1 = f32[16,27]{1,0:T(8,128)S(1)} copy-done((f32[16,27]{1,0:T(8,128)S(1)}, f32[16,27]{1,0:T(8,128)}, u32[]{:S(2)}) %copy-start.1) | copy-done | bytes 1752
  2.7 0.0 copy-start.2
  2.7 0.7 %copy-done.2 = s32[1,128]{1,0:T(1,128)S(1)} copy-done((s32[1,128]{1,0:T(1,128)S(1)}, s32[1,128]{1,0:T(1,128)}, u32[]{:S(2)}) %copy-start.2) | copy-done | bytes 536
  3.4 0.0 copy-start.3
  3.4 0.7 %copy-done.3 = f32[1,4]{1,0:T(1,128)S(1)} copy-done((f32[1,4]{1,0:T(1,128)S(1)}, f32[1,4]{1,0:T(1,128)}, u32[]{:S(2)}) %copy-start.3) | copy-done | bytes 40
  4.0 26.3 %shard_map.111 = (f32[8,512]{1,0:T(8,128)S(1)}, f32[1,16,128,128]{3,2,1,0:T(8,128)S(1)}, f32[1,16,128,128]{3,2,1,0:T(8,128)}, f32[1,4,128]{2,1,0:T(4,128)S(1)}) custom-call(f32[1,16,128,128]{3,2,1,0:T(8,128)} %prev_hbm.1, f32[1,16,128,128]{3,2,1,0:T(8,128)} %now_hbm.1, f32[1,4,16,128,128]{4,3,2,1,0:T(8,128)} %adj_hbm.1, f32[8,512]{1,0:T(8,128)S(1)} %copy-done, ...), custom_call_target="tpu_custom_call" | custom-call | tf_op jit(solution)/shard_map/pallas_call | solution.py:414
  30.4 0.6 %copy.17 = f32[8,512]{1,0:T(8,128)} copy(f32[8,512]{1,0:T(8,128)S(1)} %get-tuple-element.8) | data formatting | bytes 32768
  31.0 1.0 %copy.18 = f32[1,16,128,128]{3,2,1,0:T(8,128)} copy(f32[1,16,128,128]{3,2,1,0:T(8,128)S(1)} %get-tuple-element.9) | data formatting | bytes 2097152
  31.9 2.3 %copy.19 = f32[1,16,128,128]{3,2,1,0:T(8,128)} copy(f32[1,16,128,128]{3,2,1,0:T(8,128)} %get-tuple-element.10) | data formatting | bytes 2097152
  34.2 0.6 %copy.20 = f32[1,4,128]{2,1,0:T(4,128)} copy(f32[1,4,128]{2,1,0:T(4,128)S(1)} %get-tuple-element.11) | data formatting | bytes 4096
Async XLA Ops:
  1.3 0.7 %copy-start = (f32[8,512]{1,0:T(8,128)S(1)}, f32[8,512]{1,0:T(8,128)}, u32[]{:S(2)}) copy-start(f32[8,512]{1,0:T(8,128)} %cv.1) | copy-start | bytes 49156
  2.0 0.7 %copy-start.1 = (f32[16,27]{1,0:T(8,128)S(1)}, f32[16,27]{1,0:T(8,128)}, u32[]{:S(2)}) copy-start(f32[16,27]{1,0:T(8,128)} %filt.1) | copy-start | bytes 5188
  2.7 0.7 %copy-start.2 = (s32[1,128]{1,0:T(1,128)S(1)}, s32[1,128]{1,0:T(1,128)}, u32[]{:S(2)}) copy-start(s32[1,128]{1,0:T(1,128)} %rec_v.1) | copy-start | bytes 1540
  3.4 0.7 %copy-start.3 = (f32[1,4]{1,0:T(1,128)S(1)}, f32[1,4]{1,0:T(1,128)}, u32[]{:S(2)}) copy-start(f32[1,4]{1,0:T(1,128)} %wav.1) | copy-start | bytes 52
where the time goes:
time: 35.1 us; the launch traced here: 34.8 us
  Pallas kernels  26.3 us (75%)
  local copies, waits for them, and re-layouts  7.17 us (20%)
  between operations  1.3 us (4%)
    pallas_call x1, Pallas kernels, body(): pl.pallas_call(functools.partial(kernel, shots, steps), out_shape=(jax.Sh...  26.3 us
    unnamed x12, local copies, waits for them, and re-layouts  7.17 us

commit v1 on v0

--- a/solution.py
+++ b/solution.py
@@ -10,6 +10,7 @@
 coeffs = (-205.0 / 72.0, 8.0 / 5.0, -1.0 / 5.0, 8.0 / 315.0, -1.0 / 560.0)
 courant = 0.1
 HALO = 4
+GRANT = 56 * 2**20
 f32, bf16, i32 = jnp.float32, jnp.bfloat16, jnp.int32
 NT = (((1,), (1,)), ((), ()))
 TN = (((0,), (0,)), ((), ()))
@@ -34,14 +35,14 @@
 
 def kernel(
     shots, steps,
-    prev_hbm, now_hbm, adj_hbm, cv, filt, wav, src, rec_s, rec_v,
+    prev_hbm, now_hbm, adj_hbm, cv_hbm, filt_hbm, wav_hbm, src, rec_hbm,
     grad, pout, nout, traces,
     *scratch,
 ):
     fields = scratch[: steps + 2]
     adjs = scratch[steps + 2 : 2 * steps + 2]
     (
-        speed, acc, bx, by, lat, vel, velf, wown, wother, zx, xm, fhi, flo, sb,
+        cv, filt, wav, rec_s, rec_v, speed, acc, bx, by, lat, vel, velf, wown, wother, zx, xm, fhi, flo, sb,
         tmp, terms, arrived, picked, tr_own, tr_other,
         in_sem, out_sem, h_send, h_recv, v_send, v_recv, r_send, r_recv, w_sem, t_sem,
     ) = scratch[2 * steps + 2 :]
@@ -63,6 +64,14 @@
     load_adj = [
         pltpu.make_async_copy(adj_hbm.at[0, t], adjs[t], in_sem.at[2 + t]) for t in range(steps)
     ]
+    small = [
+        pltpu.make_async_copy(a, b, in_sem.at[2 + steps + n])
+        for n, (a, b) in enumerate(
+            ((cv_hbm, cv), (filt_hbm, filt), (wav_hbm, wav), (rec_hbm, rec_s), (rec_hbm, rec_v))
+        )
+    ]
+    for c in small:
+        c.start()
     load_now.start()
     load_prev.start()
     for c in load_adj:
@@ -72,6 +81,7 @@
     for k in range(1, shots):
         pl.semaphore_signal(barrier, inc=1, device_id={"shot": peer(k)}, device_id_type=MESH)
     pl.semaphore_signal(barrier, inc=1, device_id=other, device_id_type=MESH)
+    small[0].wait()
     pl.semaphore_wait(barrier, shots)
 
     def vel_copy(k, slot, to):
@@ -90,6 +100,8 @@
     )
     first_halo.start()
 
+    for c in small[1:]:
+        c.wait()
     for t in range(steps):
         fields[t + 1][pl.ds(far, HALO)] = jnp.zeros((HALO, wx, wy), f32)
     gap_x = jnp.abs(iota((wx, wx), 0) - iota((wx, wx), 1))
@@ -122,39 +134,6 @@
             value = value.astype(bf16)
             out[pl.ds(ab * wy, half_y), :] = value
             out[pl.ds(ab * wy + half_y, half_y), :] = value
-
-    vel[pl.ds(me_s, 1)] = cv[...][None]
-    for k in range(1, shots):
-        from_s = lax.rem(me_s + shots - k, shots)
-        vel_copy(k, from_s, peer(k)).wait_recv()
-    stacked = jnp.concatenate(
-        [vel[s, :, q * wy : (q + 1) * wy] for s in range(shots) for q in range(tiles)], axis=0
-    )
-    up_row, up_col = iota((wy, 2 * wy), 0), iota((wy, 2 * wy), 1)
-    up = (up_row == up_col // wy * half_y + up_col % wy // 2).astype(f32).astype(bf16)
-    fine = mm(
-        jnp.concatenate(split(stacked, 3), axis=1), jnp.concatenate([up, up, up], axis=0)
-    )
-    velf[0] = fine[:, :wy]
-    velf[1] = fine[:, wy:]
-    for z in range(zc_rows):
-        for i in range(2):
-            plane = courant * velf[i, pl.ds(z, pairs_x, stride=zc_rows), :]
-            plane = plane * plane
-            for j in range(2):
-                speed[z, pl.ds(2 * i + j, pairs_x, stride=4), :] = plane
-
-    before = vel[jnp.maximum(me_s - 1, 0), :, ncol - wy :]
-    after = vel[jnp.minimum(me_s + 1, shots - 1), :, :wy]
-    wown[0] = jnp.where(me_s > 0, before, 0.0)
-    for q in range(tiles):
-        wown[q + 1] = cv[:, q * wy : (q + 1) * wy]
-    wown[tiles + 1] = jnp.where(me_s < shots - 1, after, 0.0)
-    w_copy = pltpu.make_async_remote_copy(
-        src_ref=wown, dst_ref=wother, send_sem=w_sem.at[0], recv_sem=w_sem.at[1],
-        device_id=other, device_id_type=MESH,
-    )
-    w_copy.start()
 
     hit = src[0]
     hit_z = hit // (wx * wy) - me_d * rows
@@ -176,7 +155,7 @@
             lat[i] = along_x[:, i * wy : (i + 1) * wy] + along_y[i * wx : (i + 1) * wx]
         for r in range(0, wx, chunk):
             cut = pl.ds(r, chunk)
-            speed_cut = speed[zc, cut, :]
+            speed_cut = None if t == 0 else speed[zc, cut, :]
             spot_cut = tmp[cut, :]
             image = None
             planes = [current[z0 + k, cut, :] for k in range(2 * HALO + 2)]
@@ -185,9 +164,12 @@
                 lap = lat[i, cut, :] + spot_cut * pulse
                 for k in range(1, 5):
                     lap = lap + coeffs[k] * (planes[i + HALO + k] + planes[i + HALO - k])
-                following[z0 + i + HALO, cut, :] = (
-                    2.0 * planes[i + HALO] - earlier[z0 + i + HALO, cut, :] + speed_cut * lap
-                )
+                if t == 0:
+                    following[z0 + i + HALO, cut, :] = lap
+                else:
+                    following[z0 + i + HALO, cut, :] = (
+                        2.0 * planes[i + HALO] - earlier[z0 + i + HALO, cut, :] + speed_cut * lap
+                    )
                 term = adjs[t][z0 + i, cut, :] * lap
                 image = term if image is None else image + term
             if t == 0:
@@ -195,37 +177,108 @@
             else:
                 acc[zc, cut, :] = acc[zc, cut, :] + image
 
+    def finish(zc):
+        for i in range(2):
+            z = 2 * zc + i + HALO
+            for r in range(0, wx, chunk):
+                cut = pl.ds(r, chunk)
+                fields[2][z, cut, :] = (
+                    2.0 * fields[1][z, cut, :]
+                    - fields[0][z, cut, :]
+                    + speed[zc, cut, :] * fields[2][z, cut, :]
+                )
+
     edge_pairs = HALO // 2
     inside_pairs = rows // 2 - edge_pairs
     inside_first = me_d * edge_pairs
     edge_first = jnp.where(me_d == 0, inside_pairs, 0)
-    halo = first_halo
     sent = [first_halo]
+
+    def send_edge(t):
+        copy = pltpu.make_async_remote_copy(
+            src_ref=fields[t + 1].at[pl.ds(inner + HALO, HALO)],
+            dst_ref=fields[t + 1].at[pl.ds(far, HALO)],
+            send_sem=h_send.at[t], recv_sem=h_recv.at[t],
+            device_id=other, device_id_type=MESH,
+        )
+        copy.start()
+        sent.append(copy)
+
     load_now.wait()
+    load_adj[0].wait()
+
+    @pl.loop(0, inside_pairs)
+    def _(i):
+        pair(0, inside_first + i)
+
+    first_halo.wait_recv()
+
+    @pl.loop(0, edge_pairs)
+    def _(i):
+        pair(0, edge_first + i)
+
     load_prev.wait()
+    vel[pl.ds(me_s, 1)] = cv[...][None]
+    for k in range(1, shots):
+        from_s = lax.rem(me_s + shots - k, shots)
+        vel_copy(k, from_s, peer(k)).wait_recv()
+    stacked = jnp.concatenate(
+        [vel[s, :, q * wy : (q + 1) * wy] for s in range(shots) for q in range(tiles)], axis=0
+    )
+    up_row, up_col = iota((wy, 2 * wy), 0), iota((wy, 2 * wy), 1)
+    up = (up_row == up_col // wy * half_y + up_col % wy // 2).astype(f32).astype(bf16)
+    fine = mm(
+        jnp.concatenate(split(stacked, 3), axis=1), jnp.concatenate([up, up, up], axis=0)
+    )
+    velf[0] = fine[:, :wy]
+    velf[1] = fine[:, wy:]
+    for z in range(zc_rows):
+        for i in range(2):
+            plane = courant * velf[i, pl.ds(z, pairs_x, stride=zc_rows), :]
+            plane = plane * plane
+            for j in range(2):
+                speed[z, pl.ds(2 * i + j, pairs_x, stride=4), :] = plane
+
+    before = vel[jnp.maximum(me_s - 1, 0), :, ncol - wy :]
+    after = vel[jnp.minimum(me_s + 1, shots - 1), :, :wy]
+    wown[0] = jnp.where(me_s > 0, before, 0.0)
+    for q in range(tiles):
+        wown[q + 1] = cv[:, q * wy : (q + 1) * wy]
+    wown[tiles + 1] = jnp.where(me_s < shots - 1, after, 0.0)
+    w_copy = pltpu.make_async_remote_copy(
+        src_ref=wown, dst_ref=wother, send_sem=w_sem.at[0], recv_sem=w_sem.at[1],
+        device_id=other, device_id_type=MESH,
+    )
+    w_copy.start()
+
+    @pl.loop(0, edge_pairs)
+    def _(i):
+        finish(edge_first + i)
+
+    if steps > 1:
+        send_edge(1)
+
+    @pl.loop(0, inside_pairs)
+    def _(i):
+        finish(inside_first + i)
+
     stores = []
     for t in range(steps):
-        load_adj[t].wait()
-
-        @pl.loop(0, inside_pairs)
-        def _(i):
-            pair(t, inside_first + i)
-
-        halo.wait_recv()
-
-        @pl.loop(0, edge_pairs)
-        def _(i):
-            pair(t, edge_first + i)
-
-        if t + 1 < steps:
-            halo = pltpu.make_async_remote_copy(
-                src_ref=fields[t + 2].at[pl.ds(inner + HALO, HALO)],
-                dst_ref=fields[t + 2].at[pl.ds(far, HALO)],
-                send_sem=h_send.at[t + 1], recv_sem=h_recv.at[t + 1],
-                device_id=other, device_id_type=MESH,
-            )
-            halo.start()
-            sent.append(halo)
+        if t > 0:
+            load_adj[t].wait()
+
+            @pl.loop(0, inside_pairs)
+            def _(i):
+                pair(t, inside_first + i)
+
+            sent[t].wait_recv()
+
+            @pl.loop(0, edge_pairs)
+            def _(i):
+                pair(t, edge_first + i)
+
+            if t + 1 < steps:
+                send_edge(t + 1)
         if t + 2 >= steps:
             out = pout if t + 2 == steps else nout
             store = pltpu.make_async_copy(
@@ -239,8 +292,9 @@
     fold = jnp.concatenate([fold, fold], axis=0)
     left = iota((1, wy), 1) < half_y
     for z in range(zc_rows):
-        tmp[...] = mm(jnp.concatenate(split(acc[z], 2), axis=1), fold)
-        quarter = [tmp[pl.ds(j, pairs_x, stride=4), :] for j in range(4)]
+        fields[0][z] = mm(jnp.concatenate(split(acc[z], 2), axis=1), fold)
+    for z in range(zc_rows):
+        quarter = [fields[0][z, pl.ds(j, pairs_x, stride=4), :] for j in range(4)]
         terms[pl.ds(z, pairs_x, stride=zc_rows), :] = jnp.where(
             left, quarter[0] + quarter[1], quarter[2] + quarter[3]
         )
@@ -357,6 +411,30 @@
         c.wait()
 
 
+def store_kernel(*refs):
+    ins, outs, stages = refs[:4], refs[4:8], refs[8:12]
+    sem_in, sem_out = refs[12:]
+    loads, stores = [], []
+    for n in (1, 2, 0, 3):
+        rows = ins[n].shape[1]
+        pieces = 4 if n in (1, 2) and rows % 4 == 0 else 1
+        for c in range(pieces):
+            if n == 0:
+                parts = [ref for ref in (ins[n], stages[n], outs[n])]
+            else:
+                cut = pl.ds(c * (rows // pieces), rows // pieces)
+                parts = [ref.at[:, cut] for ref in (ins[n], stages[n], outs[n])]
+            loads.append(pltpu.make_async_copy(parts[0], parts[1], sem_in.at[n, c]))
+            stores.append(pltpu.make_async_copy(parts[1], parts[2], sem_out.at[n, c]))
+    for c in loads:
+        c.start()
+    for load, store in zip(loads, stores):
+        load.wait()
+        store.start()
+    for c in stores:
+        c.wait()
+
+
 def body(
     shots, wave_prev, wave_now, adjoint, coarse_velocity, filters, wavelet, source_cell,
     receiver_cells,
@@ -371,7 +449,7 @@
     out_x, deep = 2 * tiles + 2, 2 * zc_rows
     vmem = pl.BlockSpec(memory_space=pltpu.VMEM)
     smem = pl.BlockSpec(memory_space=pltpu.SMEM)
-    anyw = pl.BlockSpec(memory_space=pl.ANY)
+    hbm = pl.BlockSpec(memory_space=pltpu.HBM)
     trace_rows = -(-steps // 8) * 8
     dma = pltpu.SemaphoreType.DMA
     field = pltpu.VMEM((rows + 2 * HALO, wx, wy), f32)
@@ -379,6 +457,11 @@
         [field] * (steps + 2)
         + [pltpu.VMEM((rows, wx, wy), f32)] * steps
         + [
+            pltpu.VMEM((zc_rows, ncol), f32),
+            pltpu.VMEM(filters.shape, f32),
+            pltpu.SMEM(wavelet.shape, f32),
+            pltpu.SMEM(receiver_cells.shape, i32),
+            pltpu.VMEM(receiver_cells.shape, i32),
             pltpu.VMEM((zc_rows, wx, wy), f32),
             pltpu.VMEM((zc_rows, wx, wy), f32),
             pltpu.VMEM((wx, 3 * wx), bf16),
@@ -399,7 +482,7 @@
             pltpu.VMEM((steps, count, wy), f32),
             pltpu.VMEM((trace_rows, count), f32),
             pltpu.VMEM((trace_rows, count), f32),
-            dma((2 + steps,)),
+            dma((7 + steps,)),
             dma((2,)),
             dma((steps,)),
             dma((steps,)),
@@ -411,24 +494,33 @@
             dma((2,)),
         ]
     )
-    return pl.pallas_call(
+    out_shape = (
+        jax.ShapeDtypeStruct((zc_rows, ncol), f32),
+        jax.ShapeDtypeStruct(wave_prev.shape, f32),
+        jax.ShapeDtypeStruct(wave_now.shape, f32),
+        jax.ShapeDtypeStruct((1, steps, count), f32),
+    )
+    results = pl.pallas_call(
         functools.partial(kernel, shots, steps),
-        out_shape=(
-            jax.ShapeDtypeStruct((zc_rows, ncol), f32),
-            jax.ShapeDtypeStruct(wave_prev.shape, f32),
-            jax.ShapeDtypeStruct(wave_now.shape, f32),
-            jax.ShapeDtypeStruct((1, steps, count), f32),
-        ),
-        in_specs=[anyw, anyw, anyw, vmem, vmem, smem, smem, smem, vmem],
-        out_specs=(vmem, anyw, anyw, vmem),
+        out_shape=out_shape,
+        in_specs=[hbm, hbm, hbm, hbm, hbm, hbm, smem, hbm],
+        out_specs=(vmem, hbm, hbm, vmem),
         scratch_shapes=scratch,
         compiler_params=pltpu.CompilerParams(
-            collective_id=0, has_side_effects=True, vmem_limit_bytes=52 * 2**20
+            collective_id=0, has_side_effects=True, vmem_limit_bytes=GRANT
         ),
     )(
         wave_prev, wave_now, adjoint, coarse_velocity, filters, wavelet, source_cell,
-        receiver_cells, receiver_cells,
-    )
+        receiver_cells,
+    )
+    return pl.pallas_call(
+        store_kernel,
+        out_shape=out_shape,
+        in_specs=[hbm] * 4,
+        out_specs=(hbm,) * 4,
+        scratch_shapes=[pltpu.VMEM(x.shape, f32) for x in out_shape] + [dma((4, 4)), dma((4, 4))],
+        compiler_params=pltpu.CompilerParams(vmem_limit_bytes=GRANT),
+    )(*results)
 
 
 def solution(mesh):

time: 35.1 us -> 29.3 us (0.83)
  local copies, waits for them, and re-layouts: 7.17 us -> 0 us
  Pallas kernels: 26.3 us -> 27.7 us
    unnamed x12 -> x0, local copies, waits for them, and re-layouts: 7.17 us -> none
    pallas_call x1 -> x2, Pallas kernels: 26.3 us -> 27.7 us  [the longest x1 25.2 us: body(): pl.pallas_call(functools.partial(kernel, shots, steps), out_shape=out_sha...]
where the time goes in v1:
time: 29.3 us; the launch traced here: 29 us
  Pallas kernels  27.7 us (95%)
  between operations  1.29 us (4%)
    pallas_call x1, Pallas kernels, body(): pl.pallas_call(functools.partial(kernel, shots, steps), out_shape=out_sha...  25.2 us
    pallas_call x1, Pallas kernels, body(): pl.pallas_call(store_kernel, out_shape=out_shape, in_specs=[hbm] * 4, out...  2.54 us

profile of v1, /device:TPU:0, one launch (start us, length us, event | category | flops | bytes accessed | tf_op | source)
XLA Modules:
  0.0 29.0 jit_solution(12635374041471093988)
XLA Ops:
  1.3 25.2 %shard_map.111 = (f32[8,512]{1,0:T(8,128)}, f32[1,16,128,128]{3,2,1,0:T(8,128)}, f32[1,16,128,128]{3,2,1,0:T(8,128)}, f32[1,4,128]{2,1,0:T(4,128)}) custom-call(f32[1,16,128,128]{3,2,1,0:T(8,128)} %prev_hbm.1, f32[1,16,128,128]{3,2,1,0:T(8,128)} %now_hbm.1, f32[1,4,16,128,128]{4,3,2,1,0:T(8,128)} %adj_hbm.1, f32[8,512]{1,0:T(8,128)} %cv_hbm.1, ...), custom_call_target="tpu_custom_call" | custom-call | tf_op jit(solution)/shard_map/pallas_call | solution.py:503
  26.5 2.5 %shard_map.112 = (f32[8,512]{1,0:T(8,128)}, f32[1,16,128,128]{3,2,1,0:T(8,128)}, f32[1,16,128,128]{3,2,1,0:T(8,128)}, f32[1,4,128]{2,1,0:T(4,128)}) custom-call(f32[8,512]{1,0:T(8,128)} %get-tuple-element.8.refs_0_, f32[1,16,128,128]{3,2,1,0:T(8,128)} %get-tuple-element.9.refs_1_, f32[1,16,128,128]{3,2,1,0:T(8,128)} %get-tuple-element.10.refs_2_, ...), custom_call_target="tpu_custom_call" | custom-call | tf_op jit(solution)/shard_map/pallas_call | solution.py:516

commit v2 on v1

--- a/solution.py
+++ b/solution.py
@@ -143,7 +143,15 @@
     tmp[...] = spot
     chunk = 32
 
-    def pair(t, zc):
+    def pairs(t, first, count):
+        together = 2 if count % 2 == 0 else 1
+
+        @pl.loop(0, count // together)
+        def _(i):
+            for u in range(together):
+                pair(t, first + i * together + u, 2 * u)
+
+    def pair(t, zc, slot):
         current, earlier, following = fields[t + 1], fields[t], fields[t + 2]
         z0 = 2 * zc
         halves = [split(current[z0 + HALO + i], 2) for i in range(2)]
@@ -152,7 +160,7 @@
         along_x = mm(bx[...], jnp.concatenate([wide[0], wide[1], wide[0]], axis=0))
         along_y = mm(jnp.concatenate([tall[0], tall[1], tall[0]], axis=1), by[...])
         for i in range(2):
-            lat[i] = along_x[:, i * wy : (i + 1) * wy] + along_y[i * wx : (i + 1) * wx]
+            lat[slot + i] = along_x[:, i * wy : (i + 1) * wy] + along_y[i * wx : (i + 1) * wx]
         for r in range(0, wx, chunk):
             cut = pl.ds(r, chunk)
             speed_cut = None if t == 0 else speed[zc, cut, :]
@@ -161,7 +169,7 @@
             planes = [current[z0 + k, cut, :] for k in range(2 * HALO + 2)]
             for i in range(2):
                 pulse = jnp.where(hit_z == z0 + i, wav[0, t], 0.0)
-                lap = lat[i, cut, :] + spot_cut * pulse
+                lap = lat[slot + i, cut, :] + spot_cut * pulse
                 for k in range(1, 5):
                     lap = lap + coeffs[k] * (planes[i + HALO + k] + planes[i + HALO - k])
                 if t == 0:
@@ -207,15 +215,11 @@
     load_now.wait()
     load_adj[0].wait()
 
-    @pl.loop(0, inside_pairs)
-    def _(i):
-        pair(0, inside_first + i)
+    pairs(0, inside_first, inside_pairs)
 
     first_halo.wait_recv()
 
-    @pl.loop(0, edge_pairs)
-    def _(i):
-        pair(0, edge_first + i)
+    pairs(0, edge_first, edge_pairs)
 
     load_prev.wait()
     vel[pl.ds(me_s, 1)] = cv[...][None]
@@ -267,15 +271,11 @@
         if t > 0:
             load_adj[t].wait()
 
-            @pl.loop(0, inside_pairs)
-            def _(i):
-                pair(t, inside_first + i)
+            pairs(t, inside_first, inside_pairs)
 
             sent[t].wait_recv()
 
-            @pl.loop(0, edge_pairs)
-            def _(i):
-                pair(t, edge_first + i)
+            pairs(t, edge_first, edge_pairs)
 
             if t + 1 < steps:
                 send_edge(t + 1)
@@ -466,7 +466,7 @@
             pltpu.VMEM((zc_rows, wx, wy), f32),
             pltpu.VMEM((wx, 3 * wx), bf16),
             pltpu.VMEM((3 * wy, wy), bf16),
-            pltpu.VMEM((2, wx, wy), f32),
+            pltpu.VMEM((4, wx, wy), f32),
             pltpu.VMEM((shots, zc_rows, ncol), f32),
             pltpu.VMEM((2, pairs_x * zc_rows, wy), f32),
             pltpu.VMEM((tiles + 2, zc_rows, wy), f32),

time: 29.3 us -> 27.4 us (0.935)
  Pallas kernels: 27.7 us -> 25.8 us
    pallas_call x1, Pallas kernels: 25.2 us -> 23.3 us  [body(): pl.pallas_call(functools.partial(kernel, shots, steps), out_shape=out_sha...]
where the time goes in v2:
time: 27.4 us; the launch traced here: 27.1 us
  Pallas kernels  25.8 us (94%)
  between operations  1.29 us (5%)
    pallas_call x1, Pallas kernels, body(): pl.pallas_call(functools.partial(kernel, shots, steps), out_shape=out_sha...  23.3 us
    pallas_call x1, Pallas kernels, body(): pl.pallas_call(store_kernel, out_shape=out_shape, in_specs=[hbm] * 4, out...  2.54 us

profile of v2, /device:TPU:0, one launch (start us, length us, event | category | flops | bytes accessed | tf_op | source)
XLA Modules:
  0.0 27.1 jit_solution(5691722792165874131)
XLA Ops:
  1.3 23.3 %shard_map.111 = (f32[8,512]{1,0:T(8,128)}, f32[1,16,128,128]{3,2,1,0:T(8,128)}, f32[1,16,128,128]{3,2,1,0:T(8,128)}, f32[1,4,128]{2,1,0:T(4,128)}) custom-call(f32[1,16,128,128]{3,2,1,0:T(8,128)} %prev_hbm.1, f32[1,16,128,128]{3,2,1,0:T(8,128)} %now_hbm.1, f32[1,4,16,128,128]{4,3,2,1,0:T(8,128)} %adj_hbm.1, f32[8,512]{1,0:T(8,128)} %cv_hbm.1, ...), custom_call_target="tpu_custom_call" | custom-call | tf_op jit(solution)/shard_map/pallas_call | solution.py:503
  24.6 2.5 %shard_map.112 = (f32[8,512]{1,0:T(8,128)}, f32[1,16,128,128]{3,2,1,0:T(8,128)}, f32[1,16,128,128]{3,2,1,0:T(8,128)}, f32[1,4,128]{2,1,0:T(4,128)}) custom-call(f32[8,512]{1,0:T(8,128)} %get-tuple-element.8.refs_0_, f32[1,16,128,128]{3,2,1,0:T(8,128)} %get-tuple-element.9.refs_1_, f32[1,16,128,128]{3,2,1,0:T(8,128)} %get-tuple-element.10.refs_2_, ...), custom_call_target="tpu_custom_call" | custom-call | tf_op jit(solution)/shard_map/pallas_call | solution.py:516
